TPU v7x, 256 devices: a whole 4x4x8 slice. The times are simulated.
256 devices in a mesh: dimer: 8 (over y_hi, x), grid: 32 (over z, y_lo, core).
Axes of the slice: x: 4, y: 4 (y_hi: 2, y_lo: 2; y = y_hi * 2 + y_lo), z: 8, core: 2. Of those that a mesh axis runs over, the one named last changes fastest.
Arguments:
- basis_values: bfloat16 [8, 40960, 1024], P('dimer', 'grid'), may hold values from -15 to 15
- aux_values: bfloat16 [8, 40960, 2048], P('dimer', 'grid'), may hold values from -6 to 6
- factors: bfloat16 [8, 512, 128], P('dimer', 'grid'), may hold values from -0.25 to 0.25
- frag_slot: int32 [8], replicated, may hold values from 0 to 7, each once
- dimer_pairs: int32 [8, 2], P('dimer'), may hold values from 0 to 7, as said below
- counts: int32 [8, 32], P('dimer', 'grid'), may hold values from 1 to 1280, 16384 in all within a row
- weights: float32 [8, 40960], P('dimer', 'grid'), may hold values from 0.000390625 to 0.0015625
- metric_inv: float32 [8, 2048, 2048], P('dimer', 'grid'), may hold values from -1 to 1, as said below
Outputs:
- frag_fock: float32 [8, 512, 512], P('dimer', 'grid')
- coupling: float32 [8, 512, 512], P('dimer', 'grid')
Inputs may be any that keep to these rules, and one draw needn't show every extreme that they name: `dimer_pairs`: each fragment is named by exactly two dimers, and the two fragments of a dimer differ. For each dimer the 32 counts sum to 16384 and the largest equals 1280. `metric_inv`: each matrix is symmetric.
All inputs are finite; a program needn't handle non-finite values. No bound on the sum of `counts` on one device may be relied on, other than what follows from the above.
Results may differ from a plain program's by a relative error of at most 0.0029.
Values may be sent and summed in bfloat16 or wider, within the bound.
A program may use at most 64 MiB of HBM per device.

v0:
```python
import jax
import jax.numpy as jnp
from jax import lax
from jax.sharding import PartitionSpec as P

exchange_coeff = 0.9847450218426964


def split_product(vector, matrix, vector_left):
    high_part = vector.astype(jnp.bfloat16)
    high_back = lax.optimization_barrier(high_part).astype(jnp.float32)
    low_part = (vector - high_back).astype(jnp.bfloat16)
    if vector_left:
        return jnp.dot(high_part, matrix, preferred_element_type=jnp.float32) + jnp.dot(
            low_part, matrix, preferred_element_type=jnp.float32
        )
    return jnp.dot(matrix, high_part, preferred_element_type=jnp.float32) + jnp.dot(
        matrix, low_part, preferred_element_type=jnp.float32
    )


def contract(left_side, right_side):
    numbers = (((0,), (0,)), ((), ()))
    return lax.dot_general(left_side, right_side, numbers, preferred_element_type=jnp.float32)


def shards(basis_values, aux_values, factors, frag_slot, dimer_pairs, counts, weights, metric_inv):
    highest = lax.Precision.HIGHEST
    basis_rows = basis_values[0]
    aux_block = aux_values[0]
    points = basis_rows.shape[0]
    frag_basis = basis_rows.shape[1] // 2
    live_count = counts[0, 0]
    position = lax.iota(jnp.int32, points)
    live_weight = jnp.where(position < live_count, weights[0], jnp.zeros((), jnp.float32))
    gathered = lax.all_gather(factors, "dimer", axis=0, tiled=True)
    frag_ids = lax.iota(jnp.int32, frag_slot.shape[0])
    wanted = jnp.sum(
        jnp.where(frag_ids[None, :] == dimer_pairs[0][:, None], frag_slot[None, :], 0), axis=1
    )
    selector = (frag_ids[None, :] == wanted[:, None]).astype(jnp.bfloat16)
    chosen = jnp.einsum(
        "as,srk->ark", selector, gathered, preferred_element_type=jnp.float32
    ).astype(jnp.bfloat16)
    dimer_factors = lax.all_gather(chosen, "grid", axis=1, tiled=True)
    orb_first = jnp.dot(
        basis_rows[:, :frag_basis], dimer_factors[0], preferred_element_type=jnp.float32
    )
    orb_second = jnp.dot(
        basis_rows[:, frag_basis:], dimer_factors[1], preferred_element_type=jnp.float32
    )
    density = (
        jnp.sum(orb_first * orb_first, axis=1) + jnp.sum(orb_second * orb_second, axis=1)
    ) / (2.0 * dimer_factors.shape[2])
    exchange = -exchange_coeff * jnp.cbrt(density)
    weighted_density = live_weight * density
    fitted = lax.psum(split_product(weighted_density, aux_block, True), "grid")
    coef_rows = jnp.dot(metric_inv[0], fitted, precision=highest)
    coefficients = lax.all_gather(coef_rows, "grid", axis=0, tiled=True)
    coulomb = split_product(coefficients, aux_block, False)
    potential_total, weight_sum = lax.psum(
        (jnp.sum(live_weight * (coulomb + exchange)), jnp.sum(live_weight)), "grid"
    )
    average = potential_total / weight_sum
    potential = live_weight * (coulomb + exchange - average)
    weighted_basis = (basis_rows * potential[:, None]).astype(jnp.bfloat16)
    half_rows = frag_basis // lax.axis_size("grid")
    groups = 2 * half_rows * lax.axis_size("grid") // (2 * half_rows)
    first_index = jnp.int32(0) // 2
    left_first = lax.dynamic_slice_in_dim(
        weighted_basis, first_index, groups * half_rows, 1
    ).reshape(points, groups, half_rows)
    left_second = lax.dynamic_slice_in_dim(
        weighted_basis, frag_basis, groups * half_rows, 1
    ).reshape(points, groups, half_rows)
    left_side = jnp.concatenate([left_first, left_second], axis=2).reshape(
        points, 2 * half_rows * lax.axis_size("grid")
    )
    shares = lax.psum_scatter(
        contract(left_side, basis_rows), "grid", scatter_dimension=0, tiled=True
    )
    own_first = shares[:half_rows, :frag_basis]
    own_cross = shares[:half_rows, frag_basis:]
    own_second = shares[half_rows:, frag_basis:]
    is_first = (frag_ids == dimer_pairs[0, 0])[:, None, None]
    is_second = (frag_ids == dimer_pairs[0, 1])[:, None, None]
    fock_terms = jnp.where(is_first, own_first[None], jnp.zeros((), jnp.float32)) + jnp.where(
        is_second, own_second[None], jnp.zeros((), jnp.float32)
    )
    frag_fock = lax.psum_scatter(fock_terms, "dimer", scatter_dimension=0, tiled=True)
    return (frag_fock, own_cross[None])


def solution(mesh):
    placed = (
        P("dimer", "grid", None),
        P("dimer", "grid", None),
        P("dimer", "grid", None),
        P(),
        P("dimer", None),
        P("dimer", "grid"),
        P("dimer", "grid"),
        P("dimer", "grid", None),
    )
    return jax.shard_map(
        shards,
        mesh=mesh,
        in_specs=placed,
        out_specs=(P("dimer", "grid", None), P("dimer", "grid", None)),
        check_vma=False,
    )
```

profile of v0, /device:TPU:2, one launch (start us, length us, event | category | flops | bytes accessed | tf_op | source)
XLA Modules:
  0.0 475.2 jit_solution(4176700981948331173)
XLA Ops:
  8.0 3.0 copy.17
  11.0 34.4 %all_gather.9 = bf16[8,16,128]{2,1,0:T(8,128)(2,1)S(1)} all-gather(bf16[1,16,128]{2,1,0:T(8,128)(2,1)S(1)} %copy-done.4), channel_id=1, replica_groups=mesh['dimer'=8,'grid'=32] {'dimer'}, dimensions={0}, use_global_device_ids=true | all-gather | bytes 36864 | tf_op jit(solution)/shard_map/all_gather | solution.py:36
  45.3 0.2 fusion.39
  45.5 0.2 convolution_convert_fusion
  45.7 37.0 %all_gather.10 = bf16[2,512,128]{2,0,1:T(2,128)(2,1)S(1)} all-gather(bf16[2,16,128]{2,0,1:T(2,128)(2,1)S(1)} %convolution_convert_fusion), channel_id=1, replica_groups=mesh['dimer'=8,'grid'=32] {'grid'}, dimensions={1}, use_global_device_ids=true | all-gather | bytes 270336 | tf_op jit(solution)/shard_map/all_gather | solution.py:45
  82.7 0.4 fusion.44
  83.1 0.4 fusion.12
  83.5 0.4 fusion.15
  84.0 3.4 fusion.4
  87.4 0.6 copy-done.1
  88.0 0.8 fusion.6
  88.8 54.3 %psum.21 = f32[2048]{0:T(1024)S(1)} all-reduce(f32[2048]{0:T(1024)S(1)} %add.37), channel_id=1, replica_groups=mesh['dimer'=8,'grid'=32] {'grid'}, use_global_device_ids=true, to_apply=%region_3.4 | all-reduce | flops 2048 | bytes 16384 | tf_op jit(solution)/shard_map/psum | solution.py:57
  143.1 0.5 convolution_bitcast_fusion
  143.7 0.6 dynamic-slice
  144.9 0.3 dynamic-update-slice
  145.2 54.0 %all-reduce = f32[2048]{0:T(1024)S(1)} all-reduce(f32[2048]{0:T(1024)S(1)} %dynamic-update-slice), channel_id=1, replica_groups=mesh['dimer'=8,'grid'=32] {'grid'}, use_global_device_ids=true, to_apply=%add | all-reduce | flops 2048 | bytes 16384
  199.2 4.0 fusion.21
  203.2 4.0 fusion.18
  207.2 0.7 fusion.27
  207.9 53.6 %all-reduce.1 = (f32[]{:T(128)}, f32[]{:T(128)}) all-reduce(f32[]{:T(128)} %get-tuple-element.3, f32[]{:T(128)} %get-tuple-element.2), channel_id=1, replica_groups=mesh['dimer'=8,'grid'=32] {'grid'}, use_global_device_ids=true, to_apply=%region_5.6 | all-reduce | flops 2 | bytes 16 | tf_op jit(solution)/shard_map/psum | solution.py:61
  262.8 0.5 multiply_convert_fusion
  263.3 0.2 fusion.43
  263.5 0.3 pad_maximum_fusion
  263.8 1.4 copy-done.2
  265.2 4.4 fusion.8
  269.6 0.0 reduce-scatter.5.cloned.1.call-start
  269.7 0.6 fusion.45
  270.3 1.3 iota_compare_fusion.1
  271.6 119.2 %reduce-scatter.3.cloned.1.call-done = f32[32,1024]{1,0:T(8,128)} async-done(((f32[1024,1024]{1,0:T(8,128)}), f32[32,1024]{1,0:T(8,128)}) %reduce-scatter.3.cloned.1.call-update) | async-done | bytes 131088 | tf_op jit(solution)/shard_map/reduce_scatter | solution.py:79
  390.7 1.4 slice_bitcast_fusion
  392.1 0.8 select_add_fusion
  393.0 75.4 %reduce-scatter.5.cloned.1.call-done = f32[1,16,512]{2,1,0:T(8,128)} async-done(((f32[8,16,512]{2,1,0:T(8,128)}), f32[1,16,512]{2,1,0:T(8,128)}) %reduce-scatter.5.cloned.1.call-update) | async-done | bytes 32784 | tf_op jit(solution)/shard_map/reduce_scatter | solution.py:90
  (28 shorter events, 0.2 us)
Async XLA Ops:
  7.2 136.0 %copy-start = (f32[1,64,2048]{2,1,0:T(8,128)S(1)}, f32[1,64,2048]{2,1,0:T(8,128)}, u32[]{:S(2)}) copy-start(f32[1,64,2048]{2,1,0:T(8,128)} %param.15) | copy-start | bytes 1572868
  7.2 383.6 %reduce-scatter.3.cloned.1.call-start = ((), (), s32[]{:S(2)}) async-start(), calls=%async_computation.2 | async-start | bytes 4325376 | tf_op jit(solution)/shard_map/reduce_scatter | solution.py:79
  7.9 3.0 copy-start.4
  7.9 37.4 %copy-start.5 = (s32[1,2]{1,0:T(1,128)S(1)}, s32[1,2]{1,0:T(1,128)}, u32[]{:S(2)}) copy-start(s32[1,2]{1,0:T(1,128)} %param.12) | copy-start | bytes 28
  7.9 37.4 %copy-start.6 = (s32[8]{0:T(128)S(1)}, s32[8]{0:T(128)}, u32[]{:S(2)}) copy-start(s32[8]{0:T(128)} %param.11) | copy-start | bytes 100
  11.0 72.9 %copy-start.3 = (f32[1,1280]{1,0:T(1,128)S(1)}, f32[1,1280]{1,0:T(1,128)}, u32[]{:S(2)}) copy-start(f32[1,1280]{1,0:T(1,128)} %param.14) | copy-start | bytes 15364
  83.9 4.0 copy-start.1
  88.0 55.7 %copy-start.7 = (u32[256]{0:T(256)S(1)}, u32[256]{0:T(256)}, u32[]{:S(2)}) copy-start(u32[256]{0:T(256)} %constant.35) | copy-start | bytes 3076
  263.5 1.7 copy-start.2
  269.6 198.7 %reduce-scatter.5.cloned.1.call-start = ((), (), s32[]{:S(2)}) async-start(), calls=%async_computation.3 | async-start | bytes 294912 | tf_op jit(solution)/shard_map/reduce_scatter | solution.py:90
Sparse Core Ops, SparseCore 0:
  269.7 120.9 reduce-scatter.2
  395.2 73.1 reduce-scatter.4
where the time goes:
time: 476 us; the launch traced here: 475 us
  blocking collectives  233 us (49%)
  waiting for transfers between devices  195 us (41%)
  matrix products  18 us (4%)
  between operations  16.9 us (4%)
  local copies, waits for them, and re-layouts  8.46 us (2%)
    reduce_scatter x1, waiting for transfers between devices, shards(): lax.psum_scatter(contract(left_side, basis_rows), 'grid', scatter_dimensi...  119 us
    reduce_scatter x1, waiting for transfers between devices, shards(): lax.psum_scatter(fock_terms, 'dimer', scatter_dimension=0, tiled=True)  75.4 us
    psum x1, blocking collectives, shards(): fitted = lax.psum(split_product(weighted_density, aux_block, True), 'grid')  54.3 us
    unnamed x1, blocking collectives  54 us
    psum x1, blocking collectives, shards(): lax.psum((jnp.sum(live_weight * (coulomb + exchange)), jnp.sum(live_weigh...  53.6 us
    all_gather x1, blocking collectives, shards(): dimer_factors = lax.all_gather(chosen, 'grid', axis=1, tiled=True)  37 us
    all_gather x1, blocking collectives, shards(): gathered = lax.all_gather(factors, 'dimer', axis=0, tiled=True)  34.4 us
  transfers between devices with their start and end apart: 2, of which 2 were waited for; matrix products, arithmetic and copies ran while one was open for 0% of the time, Pallas kernels for 0%

commit v1 on v0

--- a/solution.py
+++ b/solution.py
@@ -54,7 +54,9 @@
     ) / (2.0 * dimer_factors.shape[2])
     exchange = -exchange_coeff * jnp.cbrt(density)
     weighted_density = live_weight * density
-    fitted = lax.psum(split_product(weighted_density, aux_block, True), "grid")
+    block = split_product(weighted_density, aux_block, True)
+    terms = lax.all_gather(block, "grid", axis=0, tiled=False)
+    fitted = terms.sum(axis=0)
     coef_rows = jnp.dot(metric_inv[0], fitted, precision=highest)
     coefficients = lax.all_gather(coef_rows, "grid", axis=0, tiled=True)
     coulomb = split_product(coefficients, aux_block, False)

time: 476 us -> 456 us (0.958)
  blocking collectives: 233 us -> 212 us
    psum x1 -> x0, blocking collectives: 54.3 us -> none  [shards(): fitted = lax.psum(split_product(weighted_density, aux_block, True), 'grid')]
    all_gather x0 -> x1, blocking collectives: none -> 31.4 us  [shards(): terms = lax.all_gather(block, 'grid', axis=0, tiled=False)]
where the time goes in v1:
time: 456 us; the launch traced here: 455 us
  blocking collectives  212 us (46%)
  waiting for transfers between devices  194 us (43%)
  matrix products  18 us (4%)
  between operations  16.9 us (4%)
  local copies, waits for them, and re-layouts  9.2 us (2%)
  other arithmetic  4.85 us (1%)
    reduce_scatter x1, waiting for transfers between devices, shards(): lax.psum_scatter(contract(left_side, basis_rows), 'grid', scatter_dimensi...  119 us
    reduce_scatter x1, waiting for transfers between devices, shards(): lax.psum_scatter(fock_terms, 'dimer', scatter_dimension=0, tiled=True)  75.2 us
    unnamed x1, blocking collectives  55.6 us
    psum x1, blocking collectives, shards(): lax.psum((jnp.sum(live_weight * (coulomb + exchange)), jnp.sum(live_weigh...  53.6 us
    all_gather x1, blocking collectives, shards(): dimer_factors = lax.all_gather(chosen, 'grid', axis=1, tiled=True)  37 us
    all_gather x1, blocking collectives, shards(): gathered = lax.all_gather(factors, 'dimer', axis=0, tiled=True)  34.4 us
    all_gather x1, blocking collectives, shards(): terms = lax.all_gather(block, 'grid', axis=0, tiled=False)  31.4 us
  transfers between devices with their start and end apart: 2, of which 2 were waited for; matrix products, arithmetic and copies ran while one was open for 0% of the time, Pallas kernels for 0%

profile of v1, /device:TPU:2, one launch (start us, length us, event | category | flops | bytes accessed | tf_op | source)
XLA Modules:
  0.0 455.1 jit_solution(7436727656651107146)
XLA Ops:
  8.0 3.0 copy.17
  11.0 34.4 %all_gather.15 = bf16[8,16,128]{2,1,0:T(8,128)(2,1)S(1)} all-gather(bf16[1,16,128]{2,1,0:T(8,128)(2,1)S(1)} %copy-done.4), channel_id=1, replica_groups=mesh['dimer'=8,'grid'=32] {'dimer'}, dimensions={0}, use_global_device_ids=true | all-gather | bytes 36864 | tf_op jit(solution)/shard_map/all_gather | solution.py:36
  45.3 0.2 fusion.39
  45.5 0.2 convolution_convert_fusion
  45.7 37.0 %all_gather.16 = bf16[2,512,128]{2,0,1:T(2,128)(2,1)S(1)} all-gather(bf16[2,16,128]{2,0,1:T(2,128)(2,1)S(1)} %convolution_convert_fusion), channel_id=1, replica_groups=mesh['dimer'=8,'grid'=32] {'grid'}, dimensions={1}, use_global_device_ids=true | all-gather | bytes 270336 | tf_op jit(solution)/shard_map/all_gather | solution.py:45
  82.7 0.4 fusion.44
  83.1 0.4 fusion.12
  83.5 0.4 fusion.15
  84.0 3.4 fusion.4
  87.4 0.6 copy-done.1
  88.0 0.8 fusion.6
  88.8 31.4 %all-gather = f32[65536]{0:T(1024)S(1)} all-gather(f32[2048]{0:T(1024)S(1)} %add.35), channel_id=2, replica_groups=mesh['dimer'=8,'grid'=32] {'grid'}, dimensions={0}, use_global_device_ids=true | all-gather | bytes 270336 | tf_op jit(solution)/shard_map/all_gather | solution.py:58
  120.2 0.7 reshape.55
  120.9 1.0 reduce_sum.57
  121.9 0.5 convolution_bitcast_fusion
  122.4 0.6 dynamic-slice
  123.7 0.3 dynamic-update-slice
  124.0 55.6 %all-reduce = f32[2048]{0:T(1024)S(1)} all-reduce(f32[2048]{0:T(1024)S(1)} %dynamic-update-slice), channel_id=1, replica_groups=mesh['dimer'=8,'grid'=32] {'grid'}, use_global_device_ids=true, to_apply=%add | all-reduce | flops 2048 | bytes 16384
  179.6 4.0 fusion.21
  183.6 4.0 fusion.18
  187.5 0.7 fusion.27
  188.2 53.6 %all-reduce.1 = (f32[]{:T(128)}, f32[]{:T(128)}) all-reduce(f32[]{:T(128)} %get-tuple-element.3, f32[]{:T(128)} %get-tuple-element.2), channel_id=1, replica_groups=mesh['dimer'=8,'grid'=32] {'grid'}, use_global_device_ids=true, to_apply=%region_5.6 | all-reduce | flops 2 | bytes 16 | tf_op jit(solution)/shard_map/psum | solution.py:63
  243.1 0.5 multiply_convert_fusion
  243.8 0.3 pad_maximum_fusion
  244.2 1.4 copy-done.2
  245.5 4.4 fusion.8
  250.0 0.6 fusion.45
  250.6 1.3 iota_compare_fusion.1
  251.9 118.9 %reduce-scatter.3.cloned.1.call-done = f32[32,1024]{1,0:T(8,128)} async-done(((f32[1024,1024]{1,0:T(8,128)}), f32[32,1024]{1,0:T(8,128)}) %reduce-scatter.3.cloned.1.call-update) | async-done | bytes 131088 | tf_op jit(solution)/shard_map/reduce_scatter | solution.py:81
  370.9 1.4 slice_bitcast_fusion
  372.3 0.8 select_add_fusion
  373.1 75.2 %reduce-scatter.5.cloned.1.call-done = f32[1,16,512]{2,1,0:T(8,128)} async-done(((f32[8,16,512]{2,1,0:T(8,128)}), f32[1,16,512]{2,1,0:T(8,128)}) %reduce-scatter.5.cloned.1.call-update) | async-done | bytes 32784 | tf_op jit(solution)/shard_map/reduce_scatter | solution.py:92
  (30 shorter events, 0.4 us)
Async XLA Ops:
  7.2 114.7 %copy-start = (f32[1,64,2048]{2,1,0:T(8,128)S(1)}, f32[1,64,2048]{2,1,0:T(8,128)}, u32[]{:S(2)}) copy-start(f32[1,64,2048]{2,1,0:T(8,128)} %param.15) | copy-start | bytes 1572868
  7.2 363.7 %reduce-scatter.3.cloned.1.call-start = ((), (), s32[]{:S(2)}) async-start(), calls=%async_computation.2 | async-start | bytes 4325376 | tf_op jit(solution)/shard_map/reduce_scatter | solution.py:81
  7.9 3.0 copy-start.4
  7.9 37.4 %copy-start.5 = (s32[1,2]{1,0:T(1,128)S(1)}, s32[1,2]{1,0:T(1,128)}, u32[]{:S(2)}) copy-start(s32[1,2]{1,0:T(1,128)} %param.12) | copy-start | bytes 28
  7.9 37.4 %copy-start.6 = (s32[8]{0:T(128)S(1)}, s32[8]{0:T(128)}, u32[]{:S(2)}) copy-start(s32[8]{0:T(128)} %param.11) | copy-start | bytes 100
  11.0 72.9 %copy-start.3 = (f32[1,1280]{1,0:T(1,128)S(1)}, f32[1,1280]{1,0:T(1,128)}, u32[]{:S(2)}) copy-start(f32[1,1280]{1,0:T(1,128)} %param.14) | copy-start | bytes 15364
  83.9 4.0 copy-start.1
  88.0 34.4 %copy-start.7 = (u32[256]{0:T(256)S(1)}, u32[256]{0:T(256)}, u32[]{:S(2)}) copy-start(u32[256]{0:T(256)} %constant.35) | copy-start | bytes 3076
  243.8 1.7 copy-start.2
  250.0 198.3 %reduce-scatter.5.cloned.1.call-start = ((), (), s32[]{:S(2)}) async-start(), calls=%async_computation.3 | async-start | bytes 294912 | tf_op jit(solution)/shard_map/reduce_scatter | solution.py:92
Sparse Core Ops, SparseCore 0:
  250.1 120.7 reduce-scatter.2
  375.3 72.9 reduce-scatter.4
